TPU v7x, 128 devices: a whole 4x4x4 slice. The times are simulated.
128 devices in a mesh: guide: 2 (over core), frame: 64 (over z, x, y).
Axes of the slice: x: 4, y: 4, z: 4, core: 2. Of those that a mesh axis runs over, the one named last changes fastest.
Arguments:
- head_labels: int32 [24], replicated, may hold values from 0 to 1, as said below
- queries: bfloat16 [2, 32768, 3072], P('guide', 'frame'), may hold values from -5 to 5
- key_heads: bfloat16 [2, 32768, 3072], P('guide', 'frame'), may hold values from -5 to 5
- value_heads: bfloat16 [2, 32768, 3072], P('guide', 'frame'), may hold values from -6 to 6
- hidden_state: bfloat16 [2, 32768, 3072], P('guide', 'frame'), may hold values from -2 to 2
- gate_scale: float32 [2, 3072], replicated, may hold values from 0.5 to 4
- out_weight: bfloat16 [3072, 3072], P(None, ('guide', 'frame')), may hold values from -0.109375 to 0.109375
- final_scale: float32 [2, 3072], replicated, may hold values from -2.5 to 2.5
- final_shift: float32 [2, 3072], replicated, may hold values from -2.5 to 2.5
- final_weight: bfloat16 [3072, 64], replicated, may hold values from -0.109375 to 0.109375
- latent: float32 [32768, 64], P('frame', 'guide'), may hold values from -6 to 6
Outputs:
- latent_next: float32 [32768, 64], P('frame', 'guide')
Inputs may be any that keep to these rules, and one draw needn't show every extreme that they name: `head_labels`: exactly 12 entries are 1; which heads they are varies from draw to draw.
All inputs are finite; a program needn't handle non-finite values.
Results may differ from a plain program's by a relative error of at most 0.005.
Values may be sent and summed in bfloat16 or wider, within the bound.
A program may use at most 128 MiB of HBM per device.

v0:
```python
import math

import jax
import jax.numpy as jnp
from jax import lax
from jax.sharding import PartitionSpec as P

H = 24
HD = 128
OUT_CH = 64
NT = 12
D = 3072


guidance = 6.0
euler_step = 0.25
norm_eps = 1e-06


def from_partner(x, axis, stride):
    return lax.ppermute(x, axis, [(i, i ^ 1 << stride) for i in range(lax.axis_size(axis))])


def softmax_round(scores):
    top = jnp.max(scores, axis=-1, keepdims=True)
    expd = jnp.exp(scores - top)
    return (expd / jnp.sum(expd, axis=-1, keepdims=True)).astype(jnp.bfloat16)


def spatial_head(trio):
    qq, kk, vv = trio
    scores = jnp.einsum("qd,kd->qk", qq, kk, preferred_element_type=jnp.float32) * (
        1.0 / math.sqrt(qq.shape[-1])
    )
    weights = softmax_round(scores)
    return jnp.einsum("qk,kd->qd", weights, vv, preferred_element_type=jnp.float32).astype(
        jnp.bfloat16
    )


def temporal_attend(qq, kk, vv):
    frames = lax.axis_size("frame")
    rows, heads, width = qq.shape
    group = rows // frames
    shape = (frames, group, heads, width)
    scores = jnp.einsum(
        "fphd,gphd->phfg", qq.reshape(shape), kk.reshape(shape), preferred_element_type=jnp.float32
    ) * (1.0 / math.sqrt(width))
    weights = softmax_round(scores)
    result = jnp.einsum(
        "phfg,gphd->fphd", weights, vv.reshape(shape), preferred_element_type=jnp.float32
    )
    return result.astype(jnp.bfloat16).reshape(rows, heads, width)


def per_device(
    head_labels,
    queries,
    key_heads,
    value_heads,
    hidden_state,
    gate_scale,
    out_weight,
    final_scale,
    final_shift,
    final_weight,
    latent,
):
    rows = queries.shape[1]
    branch = lax.axis_index("guide")
    half_ch = OUT_CH // 2
    order_s = jnp.argsort(head_labels, stable=True)[: H - NT]
    order_t = jnp.argsort(1 - head_labels, stable=True)[:NT]
    q_three = queries[0].reshape(rows, H, HD)
    k_three = key_heads[0].reshape(rows, H, HD)
    v_three = value_heads[0].reshape(rows, H, HD)
    spat_in = tuple(
        (
            jnp.swapaxes(jnp.take(view, order_s, axis=1), 0, 1)
            for view in (q_three, k_three, v_three)
        )
    )
    spatial = jnp.swapaxes(lax.map(spatial_head, spat_in), 0, 1)
    picked = tuple((jnp.take(view, order_t, axis=1) for view in (q_three, k_three, v_three)))
    result = temporal_attend(
        lax.all_to_all(picked[0], "frame", split_axis=0, concat_axis=0, tiled=True),
        lax.all_to_all(picked[1], "frame", split_axis=0, concat_axis=0, tiled=True),
        lax.all_to_all(picked[2], "frame", split_axis=0, concat_axis=0, tiled=True),
    )
    temporal = lax.all_to_all(result, "frame", split_axis=0, concat_axis=0, tiled=True)
    attended = jnp.zeros((rows, H, HD), jnp.bfloat16)
    attended = attended.at[:, order_s].set(spatial).at[:, order_t].set(temporal).reshape(rows, D)
    projected = jnp.dot(
        attended,
        lax.all_gather(out_weight, ("guide", "frame"), axis=1, tiled=True),
        preferred_element_type=jnp.float32,
    )
    gate_own = lax.dynamic_index_in_dim(gate_scale, branch, 0, keepdims=False)
    scale_own = lax.dynamic_index_in_dim(final_scale, branch, 0, keepdims=False)
    shift_own = lax.dynamic_index_in_dim(final_shift, branch, 0, keepdims=False)
    mixed = (hidden_state[0] + gate_own[None, :] * projected).astype(jnp.bfloat16)
    wide = mixed.astype(jnp.float32)
    row_mean = jnp.mean(wide, axis=-1, keepdims=True)
    row_square = jnp.mean(wide * wide, axis=-1, keepdims=True)
    normed = (wide - row_mean) * lax.rsqrt(row_square - row_mean * row_mean + norm_eps)
    modulated = (normed * (1.0 + scale_own[None, :]) + shift_own[None, :]).astype(jnp.bfloat16)
    velocity = jnp.dot(modulated, final_weight, preferred_element_type=jnp.float32)
    send_part = lax.dynamic_slice_in_dim(velocity, (1 - branch) * half_ch, half_ch, 1)
    own_part = lax.dynamic_slice_in_dim(velocity, branch * half_ch, half_ch, 1)
    partner = from_partner(send_part.astype(jnp.bfloat16), "guide", 0).astype(send_part.dtype)
    conditional = jnp.where(branch == 0, own_part, partner)
    unconditional = jnp.where(branch == 0, partner, own_part)
    guided = unconditional + guidance * (conditional - unconditional)
    return latent - euler_step * guided


def solution(mesh):
    placed = (
        P(),
        P("guide", "frame", None),
        P("guide", "frame", None),
        P("guide", "frame", None),
        P("guide", "frame", None),
        P(),
        P(None, ("guide", "frame")),
        P(),
        P(),
        P(),
        P("frame", "guide"),
    )
    return jax.shard_map(
        per_device, mesh=mesh, in_specs=placed, out_specs=P("frame", "guide"), check_vma=False
    )
```

profile of v0, /device:TPU:1, one launch (start us, length us, event | category | flops | bytes accessed | tf_op | source)
XLA Modules:
  0.0 275.0 jit_solution(16957150471580540159)
XLA Ops:
  7.3 4.7 %copy.34 = bf16[1,512,3072]{1,2,0:T(8,128)(2,1)} copy(bf16[1,512,3072]{2,1,0:T(8,128)(2,1)} %param.16) | data formatting | bytes 6291456 | tf_op args[1]
  12.0 3.5 %copy.35 = bf16[512,24,128]{2,0,1:T(8,128)(2,1)S(1)} copy(bf16[512,24,128]{0,2,1:T(8,128)(2,1)} %bitcast.62) | data formatting | bytes 6291456 | tf_op jit(solution)/shard_map/reshape;squeeze | solution.py:74
  15.4 4.7 %copy.36 = bf16[1,512,3072]{1,2,0:T(8,128)(2,1)} copy(bf16[1,512,3072]{2,1,0:T(8,128)(2,1)} %param.17) | data formatting | bytes 6291456 | tf_op args[2]
  20.1 4.7 %copy.37 = bf16[512,24,128]{2,0,1:T(8,128)(2,1)} copy(bf16[512,24,128]{0,2,1:T(8,128)(2,1)} %bitcast.63) | data formatting | bytes 6291456 | tf_op jit(solution)/shard_map/reshape;squeeze | solution.py:75
  31.3 3.9 %gather_fusion.5 = bf16[12,512,128]{2,1,0:T(8,128)(2,1)} fusion(bf16[512,24,128]{2,0,1:T(8,128)(2,1)} %copy.37, s32[1024]{0:T(1024)S(1)} %pad_clamp_fusion), kind=kCustom, calls=%fused_computation.5.clone | custom fusion | bytes 3145776 | tf_op jit(solution)/shard_map/jit(_take)/gather | solution.py:84
  35.2 4.7 %copy.38 = bf16[1,512,3072]{1,2,0:T(8,128)(2,1)} copy(bf16[1,512,3072]{2,1,0:T(8,128)(2,1)} %param.18) | data formatting | bytes 6291456 | tf_op args[3]
  39.9 4.7 %copy.39 = bf16[512,24,128]{2,0,1:T(8,128)(2,1)} copy(bf16[512,24,128]{0,2,1:T(8,128)(2,1)} %bitcast.64) | data formatting | bytes 6291456 | tf_op jit(solution)/shard_map/reshape;squeeze | solution.py:76
  44.5 4.0 %gather_fusion.3 = bf16[12,512,128]{2,1,0:T(8,128)(2,1)} fusion(bf16[512,24,128]{2,0,1:T(8,128)(2,1)} %copy.39, s32[1024]{0:T(1024)S(1)} %pad_clamp_fusion), kind=kCustom, calls=%fused_computation.3.clone | custom fusion | bytes 3145776 | tf_op jit(solution)/shard_map/jit(_take)/gather | solution.py:84
  48.6 4.6 %select_bitcast_fusion.2 = (bf16[512,12,128]{2,0,1:T(8,128)(2,1)}, bf16[512,12,128]{2,0,1:T(8,128)(2,1)S(1)}, bf16[512,12,128]{2,0,1:T(8,128)(2,1)}) fusion(bf16[12,512,128]{2,1,0:T(8,128)(2,1)} %gather_fusion.3, pred[12]{0:T(512)(128)(4,1)} %get-tuple-element.50, bf16[12,512,128]{2,1,0:T(8,128)(2,1)} %gather_fusion.4, bf16[12,512,128]{2,1,0:T(8,128)(2,1)} %gather_fusion.5), kind=kLoop, calls=%fused_computation.49 | loop fusion | flops 2359296 | bytes 9437196 | tf_op jit(solution)/shard_map/jit(_take)/select_n | solution.py:84
  55.6 12.1 %all-to-all-start.1 = ((bf16[512,12,128]{2,1,0:T(8,128)(2,1)}), bf16[512,12,128]{2,1,0:T(8,128)(2,1)}, u32[]{:S(2)}, u32[]{:S(2)}) async-start(bf16[512,12,128]{2,1,0:T(8,128)(2,1)} %copy.44), calls=%async_computation.1 | async-start | bytes 4194304 | tf_op jit(solution)/shard_map/all_to_all | solution.py:86
  67.7 3.8 %copy.47 = bf16[512,12,128]{2,1,0:T(8,128)(2,1)} copy(bf16[512,12,128]{2,0,1:T(8,128)(2,1)} %get-tuple-element.60) | data formatting | bytes 3145728 | tf_op jit(solution)/shard_map/jit(_take)/select_n | solution.py:84
  71.5 45.3 %all-to-all-done.1 = bf16[512,12,128]{2,1,0:T(8,128)(2,1)} async-done(((bf16[512,12,128]{2,1,0:T(8,128)(2,1)}), bf16[512,12,128]{2,1,0:T(8,128)(2,1)}, u32[]{:S(2)}, u32[]{:S(2)}) %all-to-all-start.1) | async-done | bytes 1572896 | tf_op jit(solution)/shard_map/all_to_all | solution.py:86
  116.8 6.5 %all-to-all-start.2 = ((bf16[512,12,128]{2,1,0:T(8,128)(2,1)}), bf16[512,12,128]{2,1,0:T(8,128)(2,1)}, u32[]{:S(2)}, u32[]{:S(2)}) async-start(bf16[512,12,128]{2,1,0:T(8,128)(2,1)} %copy.47), calls=%async_computation.2 | async-start | bytes 4194304 | tf_op jit(solution)/shard_map/all_to_all | solution.py:87
  123.3 3.8 %copy.41 = bf16[512,12,128]{2,1,0:T(8,128)(2,1)} copy(bf16[512,12,128]{2,0,1:T(8,128)(2,1)} %get-tuple-element.58) | data formatting | bytes 3145728 | tf_op jit(solution)/shard_map/jit(_take)/select_n | solution.py:84
  127.1 23.0 %all-to-all-done.2 = bf16[512,12,128]{2,1,0:T(8,128)(2,1)} async-done(((bf16[512,12,128]{2,1,0:T(8,128)(2,1)}), bf16[512,12,128]{2,1,0:T(8,128)(2,1)}, u32[]{:S(2)}, u32[]{:S(2)}) %all-to-all-start.2) | async-done | bytes 1572896 | tf_op jit(solution)/shard_map/all_to_all | solution.py:87
  150.1 6.8 %all-to-all-start = ((bf16[512,12,128]{2,1,0:T(8,128)(2,1)}), bf16[512,12,128]{2,1,0:T(8,128)(2,1)}, u32[]{:S(2)}, u32[]{:S(2)}) async-start(bf16[512,12,128]{2,1,0:T(8,128)(2,1)} %copy.41), calls=%async_computation | async-start | bytes 4194304 | tf_op jit(solution)/shard_map/all_to_all | solution.py:88
  158.9 4.0 %gather_fusion.1 = bf16[12,512,128]{2,1,0:T(8,128)(2,1)} fusion(bf16[512,24,128]{2,0,1:T(8,128)(2,1)} %copy.37, s32[1024]{0:T(1024)S(1)} %pad_clamp_fusion.1), kind=kCustom, calls=%fused_computation.1.clone | custom fusion | bytes 3145776 | tf_op jit(solution)/shard_map/jit(_take)/gather | solution.py:79
  164.9 4.0 %broadcast_select_fusion = (bf16[12,512,128]{2,1,0:T(8,128)(2,1)}, bf16[12,512,128]{2,1,0:T(8,128)(2,1)S(1)}, bf16[12,512,128]{2,1,0:T(8,128)(2,1)S(1)}) fusion(bf16[12,512,128]{2,1,0:T(8,128)(2,1)} %gather_fusion.2, pred[12]{0:T(512)(128)(4,1)S(1)} %get-tuple-element.67, bf16[12,512,128]{2,1,0:T(8,128)(2,1)} %gather_fusion.1, ...), kind=kLoop, calls=%fused_computation.52 | loop fusion | flops 2359296 | bytes 9437196 | tf_op jit(solution)/shard_map/jit(_take)/select_n | solution.py:79
  168.9 4.1 %fusion.25 = f32[8,12,64,64]{2,3,1,0:T(8,128)S(1)} fusion(bf16[64,8,12,128]{3,2,1,0:T(8,128)(2,1)} %bitcast.20, bf16[64,8,12,128]{3,2,1,0:T(8,128)(2,1)} %bitcast.18), kind=kOutput, calls=%fused_computation.42 | convolution fusion | flops 100663296 | bytes 4718592 | tf_op jit(solution)/shard_map/fphd,gphd->phfg/dot_general | solution.py:46
  176.2 7.4 %all-to-all-done = bf16[512,12,128]{2,1,0:T(8,128)(2,1)} async-done(((bf16[512,12,128]{2,1,0:T(8,128)(2,1)}), bf16[512,12,128]{2,1,0:T(8,128)(2,1)}, u32[]{:S(2)}, u32[]{:S(2)}) %all-to-all-start) | async-done | bytes 1572896 | tf_op jit(solution)/shard_map/all_to_all | solution.py:88
  183.6 4.4 %fusion.31 = bf16[64,8,12,128]{3,0,2,1:T(8,128)(2,1)S(1)} fusion(f32[8,12,64,64]{2,3,1,0:T(8,128)} %get-tuple-element.65, f32[8,12,64]{2,1,0:T(8,128)} %get-tuple-element.64, bf16[64,8,12,128]{3,2,1,0:T(8,128)(2,1)} %bitcast.16), kind=kOutput, calls=%fused_computation.55 | convolution fusion | flops 102236160 | bytes 4743168 | tf_op jit(solution)/shard_map/phfg,gphd->fphd/dot_general | solution.py:50
  191.7 6.7 %all-to-all-start.3 = ((bf16[512,12,128]{2,1,0:T(8,128)(2,1)}), bf16[512,12,128]{2,1,0:T(8,128)(2,1)}, u32[]{:S(2)}, u32[]{:S(2)}) async-start(bf16[512,12,128]{2,1,0:T(8,128)(2,1)} %copy.54), calls=%async_computation.3 | async-start | bytes 4194304 | tf_op jit(solution)/shard_map/all_to_all | solution.py:90
  198.5 29.3 %while.10 = (s32[]{:T(128)}, bf16[12,512,128]{2,1,0:T(8,128)(2,1)}, bf16[12,512,128]{2,1,0:T(8,128)(2,1)S(1)}, bf16[12,512,128]{2,1,0:T(8,128)(2,1)S(1)}, bf16[12,512,128]{2,1,0:T(8,128)(2,1)}, /*index=5*/s32[]{:T(128)}) while((s32[]{:T(128)}, bf16[12,512,128]{2,1,0:T(8,128)(2,1)}, bf16[12,512,128]{2,1,0:T(8,128)(2,1)S(1)}, ...), condition=%wide.region_4.6_spmd, body=%wide.region_1.5_spmd.sunk | while | flops 136117248 | bytes 3682373 | solution.py:83
  243.1 17.1 %convert_reduce_fusion = (f32[512]{0:T(512)S(1)}, f32[512]{0:T(512)S(1)}, bf16[512,3072]{1,0:T(8,128)(2,1)}) fusion(bf16[512,3072]{0,1:T(8,128)(2,1)} %bitcast.66, bf16[3072,3072]{0,1:T(8,128)(2,1)} %all-gather.2.cloned.1.call-done, f32[3072]{0:T(1024)S(1)} %bitcast.67, bf16[1,512,3072]{2,1,0:T(8,128)(2,1)} %param.19), kind=kOutput, calls=%fused_computation.28 | convolution fusion | flops 9676259328 | bytes 28327936 | tf_op jit(solution)/shard_map/dot_general | solution.py:93
  (81 shorter events, 72.9 us)
Async XLA Ops:
  6.5 253.6 %copy-start = (bf16[3072,64]{0,1:T(8,128)(2,1)S(1)}, bf16[3072,64]{0,1:T(8,128)(2,1)}, u32[]{:S(2)}) copy-start(bf16[3072,64]{0,1:T(8,128)(2,1)} %param.24) | copy-start | bytes 1179652
  6.5 236.5 %all-gather.2.cloned.1.call-start = ((), (), s32[]{:S(2)}) async-start(), calls=%async_computation.4 | async-start | bytes 19021824 | tf_op jit(solution)/shard_map/all_gather | solution.py:95
  20.1 4.7 %copy-start.5 = (s32[24]{0:T(128)S(1)}, s32[24]{0:T(128)}, u32[]{:S(2)}) copy-start(s32[24]{0:T(128)} %param.15) | copy-start | bytes 292
  55.6 61.2 %all-to-all-start.1 = ((bf16[512,12,128]{2,1,0:T(8,128)(2,1)}), bf16[512,12,128]{2,1,0:T(8,128)(2,1)}, u32[]{:S(2)}, u32[]{:S(2)}) async-start(bf16[512,12,128]{2,1,0:T(8,128)(2,1)} %copy.44), calls=%async_computation.1 | async-start | bytes 4194304 | tf_op jit(solution)/shard_map/all_to_all | solution.py:86
  116.8 33.3 %all-to-all-start.2 = ((bf16[512,12,128]{2,1,0:T(8,128)(2,1)}), bf16[512,12,128]{2,1,0:T(8,128)(2,1)}, u32[]{:S(2)}, u32[]{:S(2)}) async-start(bf16[512,12,128]{2,1,0:T(8,128)(2,1)} %copy.47), calls=%async_computation.2 | async-start | bytes 4194304 | tf_op jit(solution)/shard_map/all_to_all | solution.py:87
  150.1 33.5 %all-to-all-start = ((bf16[512,12,128]{2,1,0:T(8,128)(2,1)}), bf16[512,12,128]{2,1,0:T(8,128)(2,1)}, u32[]{:S(2)}, u32[]{:S(2)}) async-start(bf16[512,12,128]{2,1,0:T(8,128)(2,1)} %copy.41), calls=%async_computation | async-start | bytes 4194304 | tf_op jit(solution)/shard_map/all_to_all | solution.py:88
  158.9 4.0 %copy-start.1 = (bf16[512,24,128]{2,0,1:T(8,128)(2,1)S(1)}, bf16[512,24,128]{2,0,1:T(8,128)(2,1)}, u32[]{:S(2)}) copy-start(bf16[512,24,128]{2,0,1:T(8,128)(2,1)} %copy.39) | copy-start | bytes 9437188
  191.7 42.1 %all-to-all-start.3 = ((bf16[512,12,128]{2,1,0:T(8,128)(2,1)}), bf16[512,12,128]{2,1,0:T(8,128)(2,1)}, u32[]{:S(2)}, u32[]{:S(2)}) async-start(bf16[512,12,128]{2,1,0:T(8,128)(2,1)} %copy.54), calls=%async_computation.3 | async-start | bytes 4194304 | tf_op jit(solution)/shard_map/all_to_all | solution.py:90
  243.1 17.1 %copy-start.3 = (f32[1,3072]{1,0:T(1,128)S(1)}, f32[1,3072]{1,0:T(1,128)}, u32[]{:S(2)}) copy-start(f32[1,3072]{1,0:T(1,128)} %get-tuple-element.69) | copy-start | bytes 36868
  243.1 17.1 %copy-start.4 = (f32[1,3072]{1,0:T(1,128)S(1)}, f32[1,3072]{1,0:T(1,128)}, u32[]{:S(2)}) copy-start(f32[1,3072]{1,0:T(1,128)} %get-tuple-element.70) | copy-start | bytes 36868
  260.2 7.3 %copy-start.2 = (f32[512,32]{0,1:T(8,128)S(1)}, f32[512,32]{0,1:T(8,128)}, u32[]{:S(2)}) copy-start(f32[512,32]{0,1:T(8,128)} %param.25) | copy-start | bytes 196612
  263.6 3.9 %collective-permute-start = (bf16[512,32]{0,1:T(8,128)(2,1)S(1)}, bf16[512,32]{0,1:T(8,128)(2,1)S(1)}, u32[]{:S(2)}, u32[]{:S(2)}) collective-permute-start(bf16[512,32]{0,1:T(8,128)(2,1)S(1)} %dynamic-slice_convert_fusion), channel_id=1, source_target_pairs={{0,64},{64,0},{1,65},{65,1},{2,66},{66,2},{3,67},{67,3},{4,68},{68... | collective-permute-start | bytes 98312 | tf_op jit(solution)/shard_map/ppermute | solution.py:21
Sparse Core Ops, SparseCore 0:
  10.4 109.5 all-gather.1
where the time goes:
time: 277 us; the launch traced here: 275 us
  waiting for transfers between devices  77.3 us (28%)
  local copies, waits for them, and re-layouts  72.3 us (26%)
  matrix products  55.8 us (20%)
  starting transfers between devices  35.2 us (13%)
  other arithmetic  20.7 us (7%)
  between operations  13.5 us (5%)
    all_to_all x1, waiting for transfers between devices, per_device(): lax.all_to_all(picked[0], 'frame', split_axis=0, concat_axis=0, tiled=True)  45.3 us
    dot_general x12, matrix products, spatial_head(): jnp.einsum('qk,kd->qd', weights, vv, preferred_element_type=jnp.float32)  23.2 us
    all_to_all x1, waiting for transfers between devices, per_device(): lax.all_to_all(picked[1], 'frame', split_axis=0, concat_axis=0, tiled=True)  23 us
    dot_general x1, matrix products, per_device(): jnp.dot(attended, lax.all_gather(out_weight, ('guide', 'frame'), axis=1,...  17.1 us
    unnamed x15, local copies, waits for them, and re-layouts  14.1 us
    all_to_all x1, starting transfers between devices, per_device(): lax.all_to_all(picked[0], 'frame', split_axis=0, concat_axis=0, tiled=True)  12.1 us
    select_n x3, local copies, waits for them, and re-layouts, per_device(): jnp.take(view, order_t, axis=1)  9.98 us
    gather x3, local copies, waits for them, and re-layouts, per_device(): jnp.take(view, order_t, axis=1)  9.94 us
  transfers between devices with their start and end apart: 6, of which 4 were waited for; matrix products, arithmetic and copies ran while one was open for 46% of the time, Pallas kernels for 0%

commit v1 on v0

v1 whole, which is shorter than its diff:
```python
import math

import jax
import jax.numpy as jnp
from jax import lax
from jax.experimental import pallas as pl
from jax.experimental.pallas import tpu as pltpu
from jax.sharding import PartitionSpec as P

H = 24
HD = 128
OUT_CH = 64
NT = 12
D = 3072
ROWS = 512
FRAMES = 64
HALF = D // 2
COLS = 24
GP = 16
NC = 2
JC = 3
QROWS = 3 * JC * GP
OROWS = JC * GP
PART = 1024
PLANE = 16 * COLS
MESH = pl.DeviceIdType.MESH
NTDOT = (((1,), (1,)), ((), ()))
NNDOT = (((1,), (0,)), ((), ()))

guidance = 6.0
euler_step = 0.25
norm_eps = 1e-06
SCORE_SCALE = 1.0 / math.sqrt(HD)


def dot(a, b, dims):
    return lax.dot_general(a, b, dims, preferred_element_type=jnp.float32)


def order_of(labels):
    index = jnp.arange(H, dtype=jnp.int32)
    before = jnp.sum(jnp.where(index[None, :] < index[:, None], labels[None, :], 0), axis=1)
    slot = jnp.where(labels == 0, index - before, NT + before)
    return jnp.sum(
        jnp.where(slot[None, :] == index[:, None], index[None, :], 0), axis=1, dtype=jnp.int32
    )


def lanes_of(head):
    return pl.ds(pl.multiple_of(head * HD, HD), HD)


def kernel(
    order, q_hbm, k_hbm, v_hbm, hid_hbm, w_hbm, f_ref, gate, scale, shift, out,
    qv, kv, vv, send, recv, osend, orecv, att, wsrc, wb, wch, hid, tmp, otmp, ft, consts,
    zacc, sacc, zrecv,
    load_sem, own_sem, qs_sem, qr_sem, os_sem, or_sem, w1s, w1r, w2s, w2r, w3s, w3r,
    part_s, part_r,
):
    g = lax.axis_index("guide")
    f = lax.axis_index("frame")
    z, x, y = f // 16, (f // 4) % 4, f % 4
    partner = (1 - g, f)

    def at(zz, xx, yy):
        return (g, (zz % 4) * 16 + (xx % 4) * 4 + yy % 4)

    def frame_of(i):
        a, b, c = i % 4, (i // 4) % 4, i // 16
        return ((z + a + c) % 4) * 16 + ((x + a + b) % 4) * 4 + (y + a) % 4

    def remote(src, dst, ssem, rsem, dev):
        return pltpu.make_async_remote_copy(
            src_ref=src, dst_ref=dst, send_sem=ssem, recv_sem=rsem,
            device_id=dev, device_id_type=MESH,
        )

    def wait_bytes(ref, sem):
        pltpu.make_async_copy(ref, ref, sem).wait()

    own_half = pl.ds(pl.multiple_of(g * HALF, HALF), HALF)
    other_half = pl.ds(pl.multiple_of((1 - g) * HALF, HALF), HALF)

    def load(h, carry):
        lanes = lanes_of(h)
        pltpu.make_async_copy(w_hbm.at[:, lanes], wsrc.at[h], load_sem.at[0]).start()
        for t, (src, dst) in enumerate(((q_hbm, qv), (k_hbm, kv), (v_hbm, vv))):
            pltpu.make_async_copy(src.at[0, :, lanes], dst.at[h], load_sem.at[1 + t]).start()
        return carry

    lax.fori_loop(0, H, load, 0)
    hid_in = pltpu.make_async_copy(hid_hbm.at[0, :, own_half], hid.at[g], load_sem.at[4])
    hid_in.start()

    bar = pltpu.get_barrier_semaphore()

    def greet(i, carry):
        pl.semaphore_signal(bar, inc=1, device_id=(g, frame_of(i)), device_id_type=MESH)
        return carry

    lax.fori_loop(1, FRAMES, greet, 0)
    pl.semaphore_signal(bar, inc=1, device_id=partner, device_id_type=MESH)

    wait_bytes(wsrc, load_sem.at[0])
    for part in range(3):
        def permute(i, carry, part=part):
            j = part * 8 + i
            h = order[j]
            wb[part, z, x, y, :, pl.ds(pl.multiple_of(i * HD, HD), HD)] = wsrc[h]
            return carry

        lax.fori_loop(0, 8, permute, 0)

    pl.semaphore_wait(bar, FRAMES)

    w1 = []
    for part in range(3):
        for k, step in enumerate((1, 3, 2)):
            dev = (at(z, x, y + step), at(z, x + step, y), at(z + step, x, y))[part]
            block = wb.at[part, z, x, y]
            w1.append(remote(block, block, w1s.at[part * 3 + k], w1r.at[part], dev))
    for c in w1:
        c.start()
    hid_out = remote(
        hid_hbm.at[0, :, other_half], hid.at[g], part_s.at[0], part_r.at[0], partner
    )
    hid_out.start()

    for t, ref in enumerate((qv, kv, vv)):
        wait_bytes(ref, load_sem.at[1 + t])
    for c in range(NC):
        def gather(i, carry, c=c):
            hh, jj = i // JC, i % JC
            h = order[NT + c * 2 * JC + i]
            for t, ref in enumerate((qv, kv, vv)):
                rows = pl.ds(pl.multiple_of((t * JC + jj) * GP, GP), GP)
                send[c, :, hh, rows, :] = ref[h].reshape(FRAMES // 2, GP, HD)
            return carry

        lax.fori_loop(0, 2 * JC, gather, 0)

        def post(i, carry, c=c):
            d = frame_of(i)
            remote(
                send.at[c, d // 2, d % 2], recv.at[c, f], qs_sem.at[c], qr_sem.at[c], (g, d)
            ).start()
            return carry

        lax.fori_loop(1, FRAMES, post, 0)
        pltpu.make_async_copy(send.at[c, f // 2, f % 2], recv.at[c, f], own_sem.at[c]).start()

    def softmax_av(scores, values):
        top = jnp.max(scores, axis=-1, keepdims=True)
        expd = jnp.exp((scores - top) * SCORE_SCALE)
        total = jnp.sum(expd, axis=-1, keepdims=True)
        return dot((expd * (1.0 / total)).astype(jnp.bfloat16), values, NNDOT)

    def spatial(js, carry):
        h = order[js]
        keys, values = kv[h], vv[h]
        out_lanes = pl.ds(pl.multiple_of(js * HD, HD), HD)
        for rb in range(4):
            rows = pl.ds(rb * 128, 128)
            scores = dot(qv[h, rows, :], keys, NTDOT)
            att[g, rows, out_lanes] = softmax_av(scores, values).astype(jnp.bfloat16)
        return carry

    lax.fori_loop(0, 4, spatial, 0)

    def stage2(part):
        if part == 0:
            return wb.at[0, z, x]
        if part == 1:
            return wb.at[1, z, :, y]
        return wb.at[2, :, x, y]

    w2 = []
    for part in range(3):
        wait_bytes(wb.at[part, 0, 0, pl.ds(0, 3)], w1r.at[part])
        for k, step in enumerate((1, 3, 2)):
            dev = (at(z, x + step, y), at(z + step, x, y), at(z, x, y + step))[part]
            c = remote(stage2(part), stage2(part), w2s.at[part * 3 + k], w2r.at[part], dev)
            c.start()
            w2.append(c)

    lax.fori_loop(4, NT, spatial, 0)
    half_s = att.at[g, :, pl.ds(0, HALF)]
    att_s = remote(half_s, half_s, part_s.at[1], part_r.at[1], partner)
    att_s.start()

    row_id = lax.broadcasted_iota(jnp.int32, (16, HALF), 0)
    ones_row = jnp.where(row_id == 0, 1.0, 0.0).astype(jnp.bfloat16)
    for b in range(2):
        own_scale = 1.0 + scale[pl.ds(b, 1), own_half]
        for base, who in ((0, g), (48, 1 - g)):
            chans = pl.ds(pl.multiple_of(who * 32, 32), 32)
            ft[b, pl.ds(base, 32), :] = (
                f_ref[chans, own_half].astype(jnp.float32) * own_scale
            ).astype(jnp.bfloat16)
            ft[b, pl.ds(base + 32, 16), :] = ones_row
        chans = pl.ds(pl.multiple_of(g * 32, 32), 32)
        wide = f_ref[chans, :].astype(jnp.float32)
        scaled = (wide * (1.0 + scale[pl.ds(b, 1), :])).astype(jnp.bfloat16).astype(jnp.float32)
        consts[b, 0] = jnp.broadcast_to(jnp.sum(scaled, axis=1, keepdims=True), (32, HD))
        consts[b, 1] = jnp.broadcast_to(
            jnp.sum(wide * shift[pl.ds(b, 1), :], axis=1, keepdims=True), (32, HD)
        )
    zacc[...] = jnp.zeros_like(zacc)
    sacc[...] = jnp.zeros_like(sacc)

    same = (
        lax.broadcasted_iota(jnp.int32, (128, 128), 0) // FRAMES
        == lax.broadcasted_iota(jnp.int32, (128, 128), 1) // FRAMES
    )
    for c in range(NC):
        wait_bytes(recv.at[c, pl.ds(0, FRAMES - 1)], qr_sem.at[c])
        pltpu.make_async_copy(send.at[c, f // 2, f % 2], recv.at[c, f], own_sem.at[c]).wait()

        def temporal(jj, carry, c=c):
            for t in range(3):
                rows = pl.ds(pl.multiple_of((t * JC + jj) * GP, GP), GP)
                tmp[t] = recv[c, :, rows, :].reshape(FRAMES * GP, HD).astype(jnp.float32)

            def two(t, pair):
                return jnp.concatenate(
                    [
                        tmp[t, pl.ds(2 * pair + i, FRAMES, stride=GP), :].astype(jnp.bfloat16)
                        for i in range(2)
                    ],
                    axis=0,
                )

            for pair in range(GP // 2):
                scores = jnp.where(same, dot(two(0, pair), two(1, pair), NTDOT), -1e30)
                result = softmax_av(scores, two(2, pair))
                for i in range(2):
                    otmp[pl.ds(2 * pair + i, FRAMES, stride=GP), :] = result[
                        i * FRAMES : (i + 1) * FRAMES
                    ]
            rows = pl.ds(pl.multiple_of(jj * GP, GP), GP)
            osend[c, :, rows, :] = otmp[...].astype(jnp.bfloat16).reshape(FRAMES, GP, HD)
            return carry

        lax.fori_loop(0, JC, temporal, 0)

        def reply(i, carry, c=c):
            d = frame_of(i)
            remote(
                osend.at[c, d], orecv.at[c, f // 2, f % 2], os_sem.at[c], or_sem.at[c], (g, d)
            ).start()
            return carry

        lax.fori_loop(1, FRAMES, reply, 0)
        pltpu.make_async_copy(
            osend.at[c, f], orecv.at[c, f // 2, f % 2], own_sem.at[NC + c]
        ).start()

    for part in range(3):
        wait_bytes(wb.at[part, 0, pl.ds(0, 3)], w2r.at[part])

    def plane_of(r):
        return (z + jnp.where(r == 2, 3, jnp.where(r == 3, 2, r))) % 4

    def neighbour(part, step):
        return (at(z + step, x, y), at(z, x, y + step), at(z, x + step, y))[part]

    def piece(part, r, step, keep):
        if part == 0:
            return wb.at[0, (z + step) % 4, r, keep]
        if part == 1:
            return wb.at[1, plane_of(r), keep, (y + step) % 4]
        return wb.at[2, plane_of(r), (x + step) % 4, keep]

    whole, first, last = pl.ds(0, 4), pl.ds(0, 2), pl.ds(2, 2)

    def direct(part, r, way):
        ref = piece(part, r, 0, whole)
        return remote(
            ref, ref, w3s.at[part, r, way], w3r.at[part, r, way],
            neighbour(part, (1, 3)[way]),
        )

    def forward(part, r, way):
        ref = piece(part, r, (3, 1)[way], (first, last)[way])
        return remote(
            ref, ref, w3s.at[part, r, 2 + way], w3r.at[part, r, 2 + way],
            neighbour(part, (1, 3)[way]),
        )

    def arrived(part, r):
        for way in range(2):
            wait_bytes(piece(part, r, (3, 1)[way], whole), w3r.at[part, r, way])

    def arrived_far(part, r):
        for way in range(2):
            wait_bytes(piece(part, r, 2, (first, last)[way]), w3r.at[part, r, 2 + way])

    def post_direct(part, r):
        for way in range(2):
            direct(part, r, way).start()

    def pass_on(part, r):
        arrived(part, r)
        for way in range(2):
            forward(part, r, way).start()

    for r in range(2):
        for part in range(3):
            post_direct(part, r)
    for r in range(2, 4):
        post_direct(0, r)

    for c in range(NC):
        wait_bytes(osend.at[c, pl.ds(0, FRAMES - 1)], or_sem.at[c])
        pltpu.make_async_copy(
            osend.at[c, f], orecv.at[c, f // 2, f % 2], own_sem.at[NC + c]
        ).wait()
        for i in range(2 * JC):
            hh, jj = i // JC, i % JC
            lanes = pl.ds(HALF + (c * 2 * JC + i) * HD, HD)
            att[g, :, lanes] = orecv[c, :, hh, pl.ds(jj * GP, GP), :].reshape(ROWS, HD)
        block = att.at[g, :, pl.ds(HALF + c * 2 * JC * HD, 2 * JC * HD)]
        remote(block, block, part_s.at[2 + c], part_r.at[2 + c], partner).start()

    hid_in.wait()
    hid_out.wait_recv()
    att_s.wait_recv()
    for c in range(NC):
        block = att.at[g, :, pl.ds(HALF + c * 2 * JC * HD, 2 * JC * HD)]
        remote(block, block, part_s.at[2 + c], part_r.at[2 + c], partner).wait_recv()

    for part in (1, 2):
        pass_on(part, 0)
        post_direct(part, 2)
    for r in range(2):
        pass_on(0, r)

    def project(r, carry):
        @pl.when(r < 4)
        def _():
            for part in (1, 2):
                pass_on(part, r)

        @pl.when(r == 1)
        def _():
            for part in (1, 2):
                post_direct(part, 3)

        @pl.when(r == 2)
        def _():
            for k in range(2, 4):
                pass_on(0, k)

        for part in (1, 2):
            arrived_far(part, r - 1)

        @pl.when(r == 4)
        def _():
            for k in range(4):
                arrived_far(0, k)

        plane = plane_of(r - 1)
        for s in range(16):
            for part in range(3):
                wch[pl.ds(s * COLS, COLS), pl.ds(part * PART, PART)] = wb[
                    part, plane, s // 4, s % 4
                ]
        near = pl.ds(pl.multiple_of(plane * PLANE, HD), PLANE)
        far = pl.ds(pl.multiple_of(g * HALF + plane * PLANE, HD), PLANE)
        for b in range(2):
            projected = dot(att[b], wch[...], NTDOT)
            mixed = (
                hid[b, :, near].astype(jnp.float32) + gate[pl.ds(b, 1), far] * projected
            ).astype(jnp.bfloat16)
            rows = pl.ds(b * ROWS, ROWS)
            zacc[:, rows] += dot(ft[b, :, near], mixed, NTDOT)
            wide = mixed.astype(jnp.float32)
            square = wide * wide
            sacc[rows, :] += square[:, :128] + square[:, 128:256] + square[:, 256:]
        return carry

    lax.fori_loop(1, 5, project, 0)

    squares = jnp.sum(jnp.transpose(sacc[...]), axis=0, keepdims=True)
    for base in (32, 80):
        block = zacc[pl.ds(base, 8), :]
        pick = lax.broadcasted_iota(jnp.int32, block.shape, 0) == 1
        zacc[pl.ds(base, 8), :] = jnp.where(pick, squares, block)
    zsend = remote(zacc.at[pl.ds(48, 48)], zrecv, part_s.at[4], part_r.at[4], partner)
    zsend.start()
    zsend.wait_recv()
    velocity = []
    for b in range(2):
        cols = pl.ds(b * ROWS, ROWS)
        total = zacc[pl.ds(0, 40), cols] + zrecv[pl.ds(0, 40), cols]
        mean = total[32:33] * (1.0 / D)
        square = total[33:34] * (1.0 / D)
        velocity.append(
            (total[:32] - mean * consts[b, 0, :, 0:1])
            * lax.rsqrt(square - mean * mean + norm_eps)
            + consts[b, 1, :, 0:1]
        )
    out[...] = velocity[1] + guidance * (velocity[0] - velocity[1])

    zsend.wait_send()
    hid_out.wait_send()
    att_s.wait_send()
    for c in w1 + w2:
        c.wait_send()
    for c in range(NC):
        block = att.at[g, :, pl.ds(HALF + c * 2 * JC * HD, 2 * JC * HD)]
        remote(block, block, part_s.at[2 + c], part_r.at[2 + c], partner).wait_send()
        wait_bytes(recv.at[c, pl.ds(0, FRAMES - 1)], qs_sem.at[c])
        wait_bytes(osend.at[c, pl.ds(0, FRAMES - 1)], os_sem.at[c])

    def drain(r, carry):
        for part in range(3):
            for way in range(2):
                direct(part, r, way).wait_send()
                forward(part, r, way).wait_send()
        return carry

    lax.fori_loop(0, 4, drain, 0)


def per_device(
    head_labels,
    queries,
    key_heads,
    value_heads,
    hidden_state,
    gate_scale,
    out_weight,
    final_scale,
    final_shift,
    final_weight,
    latent,
):
    anyspace = pl.BlockSpec(memory_space=pl.ANY)
    vmem = pl.BlockSpec(memory_space=pltpu.VMEM)
    smem = pl.BlockSpec(memory_space=pltpu.SMEM)
    bf16, f32 = jnp.bfloat16, jnp.float32
    dma = pltpu.SemaphoreType.DMA
    guided = pl.pallas_call(
        kernel,
        out_shape=jax.ShapeDtypeStruct((OUT_CH // 2, ROWS), f32),
        in_specs=[smem] + [anyspace] * 5 + [vmem] * 4,
        out_specs=vmem,
        scratch_shapes=[
            pltpu.VMEM((H, ROWS, HD), bf16),
            pltpu.VMEM((H, ROWS, HD), bf16),
            pltpu.VMEM((H, ROWS, HD), bf16),
            pltpu.VMEM((NC, FRAMES // 2, 2, QROWS, HD), bf16),
            pltpu.VMEM((NC, FRAMES, QROWS, HD), bf16),
            pltpu.VMEM((NC, FRAMES, OROWS, HD), bf16),
            pltpu.VMEM((NC, FRAMES // 2, 2, OROWS, HD), bf16),
            pltpu.VMEM((2, ROWS, D), bf16),
            pltpu.VMEM((H, COLS, HD), bf16),
            pltpu.VMEM((3, 4, 4, 4, COLS, PART), bf16),
            pltpu.VMEM((PLANE, D), bf16),
            pltpu.VMEM((2, ROWS, HALF), bf16),
            pltpu.VMEM((3, FRAMES * GP, HD), f32),
            pltpu.VMEM((FRAMES * GP, HD), f32),
            pltpu.VMEM((2, 96, HALF), bf16),
            pltpu.VMEM((2, 2, 32, HD), f32),
            pltpu.VMEM((96, 2 * ROWS), f32),
            pltpu.VMEM((2 * ROWS, HD), f32),
            pltpu.VMEM((48, 2 * ROWS), f32),
            dma((5,)), dma((2 * NC,)),
            dma((NC,)), dma((NC,)), dma((NC,)), dma((NC,)),
            dma((9,)), dma((3,)), dma((9,)), dma((3,)),
            dma((3, 4, 4)), dma((3, 4, 4)),
            dma((5,)), dma((5,)),
        ],
        compiler_params=pltpu.CompilerParams(
            collective_id=0, has_side_effects=True, vmem_limit_bytes=62 * 2**20
        ),
        cost_estimate=pl.CostEstimate(
            flops=16 * 10**9, bytes_accessed=20 * 10**6, transcendentals=4 * 10**6
        ),
        name="guided_layer",
    )(
        order_of(head_labels), queries, key_heads, value_heads, hidden_state,
        out_weight.T, final_weight.T, gate_scale, final_scale, final_shift,
    )
    return (latent.T - euler_step * guided).T


def solution(mesh):
    placed = (
        P(),
        P("guide", "frame", None),
        P("guide", "frame", None),
        P("guide", "frame", None),
        P("guide", "frame", None),
        P(),
        P(None, ("guide", "frame")),
        P(),
        P(),
        P(),
        P("frame", "guide"),
    )
    return jax.shard_map(
        per_device, mesh=mesh, in_specs=placed, out_specs=P("frame", "guide"), check_vma=False
    )
```

time: 277 us -> 132 us (0.48)
  Pallas kernels: 0 us -> 128 us
  waiting for transfers between devices: 77.3 us -> 0 us
  local copies, waits for them, and re-layouts: 72.3 us -> 0.01 us
  matrix products: 55.8 us -> 0 us
  starting transfers between devices: 35.2 us -> 0 us
  other arithmetic: 20.7 us -> 3.54 us
  between operations: 13.5 us -> 0.02 us
    pallas_call x0 -> x1, Pallas kernels: none -> 128 us  [per_device(): pl.pallas_call(kernel, out_shape=jax.ShapeDtypeStruct((OUT_CH // 2, ROWS)...]
    all_to_all x4 -> x0, waiting for transfers between devices: 75.8 us -> none  [the longest x1 45.3 us: per_device(): lax.all_to_all(picked[0], 'frame', split_axis=0, concat_axis=0, tiled=True)]
    dot_general x28 -> x0, matrix products: 55.8 us -> none  [the longest x12 23.2 us: spatial_head(): jnp.einsum('qk,kd->qd', weights, vv, preferred_element_type=jnp.float32)]
    all_to_all x4 -> x0, starting transfers between devices: 32.1 us -> none  [the longest x1 12.1 us: per_device(): lax.all_to_all(picked[0], 'frame', split_axis=0, concat_axis=0, tiled=True)]
    gather x6 -> x0, local copies, waits for them, and re-layouts: 17.9 us -> none  [the longest x3 9.94 us: per_device(): jnp.take(view, order_t, axis=1)]
    unnamed x15 -> x2, local copies, waits for them, and re-layouts: 14.1 us -> 0.01 us
    another operation x3 -> x0, local copies, waits for them, and re-layouts: 12.8 us -> none  [the longest x1 4.7 us: per_device(): k_three = key_heads[0].reshape(rows, H, HD)]
    select_n x3 -> x0, local copies, waits for them, and re-layouts: 9.98 us -> none  [per_device(): jnp.take(view, order_t, axis=1)]
  transfers between devices with their start and end apart: 6 -> 0, of which waited for: 4 -> 0; matrix products, arithmetic and copies ran while one was open for 46% -> 0% of each run, Pallas kernels for 0% -> 0%
where the time goes in v1:
time: 132 us; the launch traced here: 131 us
  Pallas kernels  128 us (97%)
  other arithmetic  3.54 us (3%)
    pallas_call x1, Pallas kernels, per_device(): pl.pallas_call(kernel, out_shape=jax.ShapeDtypeStruct((OUT_CH // 2, ROWS)...  128 us

profile of v1, /device:TPU:1, one launch (start us, length us, event | category | flops | bytes accessed | tf_op | source)
XLA Modules:
  0.0 131.4 jit_solution(321510120337984762)
XLA Ops:
  0.0 0.8 select_reduce_fusion.1
  0.8 0.7 compare_select_fusion
  1.4 0.6 select_reduce_fusion.order
  2.1 0.0 copy-start
  2.1 127.8 %guided_layer.1 = f32[32,512]{1,0:T(8,128)} custom-call(s32[24]{0:T(128)} %select_reduce_fusion.order, bf16[1,512,3072]{2,1,0:T(8,128)(2,1)} %q_hbm.1, bf16[1,512,3072]{2,1,0:T(8,128)(2,1)} %k_hbm.1, bf16[1,512,3072]{2,1,0:T(8,128)(2,1)} %v_hbm.1, bf16[1,512,3072]{2,1,0:T(8,128)(2,1)} %hid_hbm.1, bf16[24,3072]{1,0:T(8,128)(2,1)} %bitcast.9, ...), custom_call_target="tpu_custom_call" | custom-call | flops 16000000000 | bytes 20000000 | tf_op jit(solution)/shard_map/guided_layer/pallas_call | solution.py:444
  129.9 0.0 copy-done
  129.9 1.5 %fusion = f32[512,32]{0,1:T(8,128)} fusion(f32[512,32]{0,1:T(8,128)S(1)} %copy-done, f32[32,512]{1,0:T(8,128)} %guided_layer.1), kind=kLoop, calls=%fused_computation.1 | loop fusion | flops 32768 | bytes 196608 | tf_op jit(solution)/shard_map/transpose | solution.py:486
Async XLA Ops:
  2.1 127.8 %copy-start = (f32[512,32]{0,1:T(8,128)S(1)}, f32[512,32]{0,1:T(8,128)}, u32[]{:S(2)}) copy-start(f32[512,32]{0,1:T(8,128)} %param.21) | copy-start | bytes 196612

commit v2 on v1

--- a/solution.py
+++ b/solution.py
@@ -37,25 +37,16 @@
     return lax.dot_general(a, b, dims, preferred_element_type=jnp.float32)
 
 
-def order_of(labels):
-    index = jnp.arange(H, dtype=jnp.int32)
-    before = jnp.sum(jnp.where(index[None, :] < index[:, None], labels[None, :], 0), axis=1)
-    slot = jnp.where(labels == 0, index - before, NT + before)
-    return jnp.sum(
-        jnp.where(slot[None, :] == index[:, None], index[None, :], 0), axis=1, dtype=jnp.int32
-    )
-
-
 def lanes_of(head):
     return pl.ds(pl.multiple_of(head * HD, HD), HD)
 
 
 def kernel(
-    order, q_hbm, k_hbm, v_hbm, hid_hbm, w_hbm, f_ref, gate, scale, shift, out,
+    labels, q_hbm, k_hbm, v_hbm, hid_hbm, w_hbm, f_ref, gate, scale, shift, out,
     qv, kv, vv, send, recv, osend, orecv, att, wsrc, wb, wch, hid, tmp, otmp, ft, consts,
     zacc, sacc, zrecv,
     load_sem, own_sem, qs_sem, qr_sem, os_sem, or_sem, w1s, w1r, w2s, w2r, w3s, w3r,
-    part_s, part_r,
+    part_s, part_r, step_sem, order, perm,
 ):
     g = lax.axis_index("guide")
     f = lax.axis_index("frame")
@@ -63,11 +54,11 @@
     partner = (1 - g, f)
 
     def at(zz, xx, yy):
-        return (g, (zz % 4) * 16 + (xx % 4) * 4 + yy % 4)
+        return (g, lax.rem(zz, 4) * 16 + lax.rem(xx, 4) * 4 + lax.rem(yy, 4))
 
     def frame_of(i):
-        a, b, c = i % 4, (i // 4) % 4, i // 16
-        return ((z + a + c) % 4) * 16 + ((x + a + b) % 4) * 4 + (y + a) % 4
+        a, b, c = lax.rem(i, 4), lax.rem(lax.div(i, 4), 4), lax.div(i, 16)
+        return lax.rem(z + a + c, 4) * 16 + lax.rem(x + a + b, 4) * 4 + lax.rem(y + a, 4)
 
     def remote(src, dst, ssem, rsem, dev):
         return pltpu.make_async_remote_copy(
@@ -81,25 +72,43 @@
     own_half = pl.ds(pl.multiple_of(g * HALF, HALF), HALF)
     other_half = pl.ds(pl.multiple_of((1 - g) * HALF, HALF), HALF)
 
+    bar = pltpu.get_barrier_semaphore()
+    pl.semaphore_signal(bar, inc=1, device_id=partner, device_id_type=MESH)
+    for k in range(1, 4):
+        pl.semaphore_signal(bar, inc=1, device_id=at(z + k, x, y), device_id_type=MESH)
+
+    def greet(i, carry):
+        dev = at(z, x + lax.div(i, 4), y + lax.rem(i, 4))
+        pl.semaphore_signal(bar, inc=1, device_id=dev, device_id_type=MESH)
+        return carry
+
+    lax.fori_loop(1, 16, greet, 0)
+
+    def load_w(h, carry):
+        pltpu.make_async_copy(w_hbm.at[:, lanes_of(h)], wsrc.at[h], load_sem.at[0]).start()
+        return carry
+
     def load(h, carry):
         lanes = lanes_of(h)
-        pltpu.make_async_copy(w_hbm.at[:, lanes], wsrc.at[h], load_sem.at[0]).start()
         for t, (src, dst) in enumerate(((q_hbm, qv), (k_hbm, kv), (v_hbm, vv))):
             pltpu.make_async_copy(src.at[0, :, lanes], dst.at[h], load_sem.at[1 + t]).start()
         return carry
 
+    lax.fori_loop(0, H, load_w, 0)
     lax.fori_loop(0, H, load, 0)
     hid_in = pltpu.make_async_copy(hid_hbm.at[0, :, own_half], hid.at[g], load_sem.at[4])
     hid_in.start()
 
-    bar = pltpu.get_barrier_semaphore()
-
-    def greet(i, carry):
-        pl.semaphore_signal(bar, inc=1, device_id=(g, frame_of(i)), device_id_type=MESH)
-        return carry
-
-    lax.fori_loop(1, FRAMES, greet, 0)
-    pl.semaphore_signal(bar, inc=1, device_id=partner, device_id_type=MESH)
+    slots, ones = [], jnp.int32(0)
+    for h in range(H):
+        slots.append(jnp.where(labels[h] == 0, h - ones, NT + ones))
+        ones = ones + labels[h]
+    for j in range(H):
+        found = jnp.int32(0)
+        for h in range(j % NT, j % NT + NT + 1):
+            if h < H:
+                found = jnp.where(slots[h] == j, jnp.int32(h), found)
+        order[j] = found
 
     wait_bytes(wsrc, load_sem.at[0])
     for part in range(3):
@@ -111,7 +120,7 @@
 
         lax.fori_loop(0, 8, permute, 0)
 
-    pl.semaphore_wait(bar, FRAMES)
+    pl.semaphore_wait(bar, 19)
 
     w1 = []
     for part in range(3):
@@ -121,6 +130,9 @@
             w1.append(remote(block, block, w1s.at[part * 3 + k], w1r.at[part], dev))
     for c in w1:
         c.start()
+
+    for k in range(1, 4):
+        pl.semaphore_signal(step_sem, inc=1, device_id=at(z + k, x, y), device_id_type=MESH)
     hid_out = remote(
         hid_hbm.at[0, :, other_half], hid.at[g], part_s.at[0], part_r.at[0], partner
     )
@@ -128,62 +140,75 @@
 
     for t, ref in enumerate((qv, kv, vv)):
         wait_bytes(ref, load_sem.at[1 + t])
-    for c in range(NC):
-        def gather(i, carry, c=c):
-            hh, jj = i // JC, i % JC
+
+    def gather(c):
+        def body(i, carry):
+            hh, jj = lax.div(i, JC), lax.rem(i, JC)
             h = order[NT + c * 2 * JC + i]
             for t, ref in enumerate((qv, kv, vv)):
                 rows = pl.ds(pl.multiple_of((t * JC + jj) * GP, GP), GP)
                 send[c, :, hh, rows, :] = ref[h].reshape(FRAMES // 2, GP, HD)
             return carry
 
-        lax.fori_loop(0, 2 * JC, gather, 0)
-
-        def post(i, carry, c=c):
+        lax.fori_loop(0, 2 * JC, body, 0)
+
+    def post(c):
+        def body(i, carry):
             d = frame_of(i)
             remote(
-                send.at[c, d // 2, d % 2], recv.at[c, f], qs_sem.at[c], qr_sem.at[c], (g, d)
+                send.at[c, lax.div(d, 2), lax.rem(d, 2)], recv.at[c, f],
+                qs_sem.at[c], qr_sem.at[c], (g, d),
             ).start()
             return carry
 
-        lax.fori_loop(1, FRAMES, post, 0)
+        lax.fori_loop(1, FRAMES, body, 0)
         pltpu.make_async_copy(send.at[c, f // 2, f % 2], recv.at[c, f], own_sem.at[c]).start()
 
-    def softmax_av(scores, values):
-        top = jnp.max(scores, axis=-1, keepdims=True)
-        expd = jnp.exp((scores - top) * SCORE_SCALE)
-        total = jnp.sum(expd, axis=-1, keepdims=True)
-        return dot((expd * (1.0 / total)).astype(jnp.bfloat16), values, NNDOT)
+    def shards(part, step, keep):
+        if part == 0:
+            return wb.at[0, z, (x + step) % 4, keep]
+        if part == 1:
+            return wb.at[1, (z + step) % 4, keep, y]
+        return wb.at[2, keep, x, (y + step) % 4]
+
+    whole, first, last = pl.ds(0, 4), pl.ds(0, 2), pl.ds(2, 2)
+
+    def second(part, step):
+        return (at(z, x + step, y), at(z + step, x, y), at(z, x, y + step))[part]
+
+    gather(0)
+
+    gather(1)
+    pl.semaphore_wait(step_sem, 3)
+    post(0)
+    post(1)
+    w2 = []
+    for part in range(3):
+        wait_bytes(wb.at[part, 0, 0, pl.ds(0, 3)], w1r.at[part])
+        ref = shards(part, 0, whole)
+        for k, step in enumerate((1, 3, 2)):
+            c = remote(ref, ref, w2s.at[part * 3 + k], w2r.at[part], second(part, step))
+            c.start()
+            w2.append(c)
+
+
+    def softmax(blocks):
+        tops = [jnp.max(v, axis=-1, keepdims=True) for v in blocks]
+        expd = [jnp.exp((v - top) * SCORE_SCALE) for v, top in zip(blocks, tops)]
+        shares = [1.0 / jnp.sum(v, axis=-1, keepdims=True) for v in expd]
+        return [(v * share).astype(jnp.bfloat16) for v, share in zip(expd, shares)]
 
     def spatial(js, carry):
         h = order[js]
         keys, values = kv[h], vv[h]
         out_lanes = pl.ds(pl.multiple_of(js * HD, HD), HD)
-        for rb in range(4):
-            rows = pl.ds(rb * 128, 128)
-            scores = dot(qv[h, rows, :], keys, NTDOT)
-            att[g, rows, out_lanes] = softmax_av(scores, values).astype(jnp.bfloat16)
+        blocks = [pl.ds(rb * 128, 128) for rb in range(4)]
+        weights = softmax([dot(qv[h, rows, :], keys, NTDOT) for rows in blocks])
+        for rows, weight in zip(blocks, weights):
+            att[g, rows, out_lanes] = dot(weight, values, NNDOT).astype(jnp.bfloat16)
         return carry
 
-    lax.fori_loop(0, 4, spatial, 0)
-
-    def stage2(part):
-        if part == 0:
-            return wb.at[0, z, x]
-        if part == 1:
-            return wb.at[1, z, :, y]
-        return wb.at[2, :, x, y]
-
-    w2 = []
-    for part in range(3):
-        wait_bytes(wb.at[part, 0, 0, pl.ds(0, 3)], w1r.at[part])
-        for k, step in enumerate((1, 3, 2)):
-            dev = (at(z, x + step, y), at(z + step, x, y), at(z, x, y + step))[part]
-            c = remote(stage2(part), stage2(part), w2s.at[part * 3 + k], w2r.at[part], dev)
-            c.start()
-            w2.append(c)
-
-    lax.fori_loop(4, NT, spatial, 0)
+    lax.fori_loop(0, NT, spatial, 0)
     half_s = att.at[g, :, pl.ds(0, HALF)]
     att_s = remote(half_s, half_s, part_s.at[1], part_r.at[1], partner)
     att_s.start()
@@ -208,56 +233,6 @@
     zacc[...] = jnp.zeros_like(zacc)
     sacc[...] = jnp.zeros_like(sacc)
 
-    same = (
-        lax.broadcasted_iota(jnp.int32, (128, 128), 0) // FRAMES
-        == lax.broadcasted_iota(jnp.int32, (128, 128), 1) // FRAMES
-    )
-    for c in range(NC):
-        wait_bytes(recv.at[c, pl.ds(0, FRAMES - 1)], qr_sem.at[c])
-        pltpu.make_async_copy(send.at[c, f // 2, f % 2], recv.at[c, f], own_sem.at[c]).wait()
-
-        def temporal(jj, carry, c=c):
-            for t in range(3):
-                rows = pl.ds(pl.multiple_of((t * JC + jj) * GP, GP), GP)
-                tmp[t] = recv[c, :, rows, :].reshape(FRAMES * GP, HD).astype(jnp.float32)
-
-            def two(t, pair):
-                return jnp.concatenate(
-                    [
-                        tmp[t, pl.ds(2 * pair + i, FRAMES, stride=GP), :].astype(jnp.bfloat16)
-                        for i in range(2)
-                    ],
-                    axis=0,
-                )
-
-            for pair in range(GP // 2):
-                scores = jnp.where(same, dot(two(0, pair), two(1, pair), NTDOT), -1e30)
-                result = softmax_av(scores, two(2, pair))
-                for i in range(2):
-                    otmp[pl.ds(2 * pair + i, FRAMES, stride=GP), :] = result[
-                        i * FRAMES : (i + 1) * FRAMES
-                    ]
-            rows = pl.ds(pl.multiple_of(jj * GP, GP), GP)
-            osend[c, :, rows, :] = otmp[...].astype(jnp.bfloat16).reshape(FRAMES, GP, HD)
-            return carry
-
-        lax.fori_loop(0, JC, temporal, 0)
-
-        def reply(i, carry, c=c):
-            d = frame_of(i)
-            remote(
-                osend.at[c, d], orecv.at[c, f // 2, f % 2], os_sem.at[c], or_sem.at[c], (g, d)
-            ).start()
-            return carry
-
-        lax.fori_loop(1, FRAMES, reply, 0)
-        pltpu.make_async_copy(
-            osend.at[c, f], orecv.at[c, f // 2, f % 2], own_sem.at[NC + c]
-        ).start()
-
-    for part in range(3):
-        wait_bytes(wb.at[part, 0, pl.ds(0, 3)], w2r.at[part])
-
     def plane_of(r):
         return (z + jnp.where(r == 2, 3, jnp.where(r == 3, 2, r))) % 4
 
@@ -271,8 +246,6 @@
             return wb.at[1, plane_of(r), keep, (y + step) % 4]
         return wb.at[2, plane_of(r), (x + step) % 4, keep]
 
-    whole, first, last = pl.ds(0, 4), pl.ds(0, 2), pl.ds(2, 2)
-
     def direct(part, r, way):
         ref = piece(part, r, 0, whole)
         return remote(
@@ -304,13 +277,77 @@
         for way in range(2):
             forward(part, r, way).start()
 
-    for r in range(2):
-        for part in range(3):
-            post_direct(part, r)
-    for r in range(2, 4):
-        post_direct(0, r)
-
-    for c in range(NC):
+    def swapped(n):
+        r = lax.broadcasted_iota(jnp.int32, (n, n), 0)
+        c = lax.broadcasted_iota(jnp.int32, (n, n), 1)
+        return (lax.rem(r, GP) == lax.div(c, GP)) & (lax.div(r, GP) == lax.rem(c, GP))
+
+    perm[...] = jnp.where(swapped(GP * GP), 1.0, 0.0).astype(jnp.bfloat16)
+    row_pos = lax.rem(lax.div(lax.broadcasted_iota(jnp.int32, (128, 128), 0), GP), 2)
+    col_pos = lax.rem(lax.div(lax.broadcasted_iota(jnp.int32, (128, 128), 1), GP), 2)
+    same = row_pos == col_pos
+
+    def swap(one, two):
+        both = dot(perm[...], jnp.concatenate([one, two], axis=1), NNDOT).astype(jnp.bfloat16)
+        return both[:, :HD], both[:, HD:]
+
+    def arrive(c):
+        wait_bytes(recv.at[c, pl.ds(0, FRAMES - 1)], qr_sem.at[c])
+        pltpu.make_async_copy(send.at[c, f // 2, f % 2], recv.at[c, f], own_sem.at[c]).wait()
+
+    def attend(c):
+        def temporal(jj, carry):
+            def block(t, fb):
+                rows = pl.ds(pl.multiple_of((t * JC + jj) * GP, GP), GP)
+                return recv[c, pl.ds(fb * GP, GP), rows, :].reshape(GP * GP, HD)
+
+            for one, two in [((0, fb), (1, fb)) for fb in range(4)] + [
+                ((2, 0), (2, 1)), ((2, 2), (2, 3))
+            ]:
+                for (t, fb), val in zip((one, two), swap(block(*one), block(*two))):
+                    tmp[t, fb] = val.reshape(GP, GP, HD)
+
+            def pair_of(t, pair):
+                return tmp[t, :, pl.ds(2 * pair, 2), :, :].reshape(128, HD)
+
+            pairs = range(GP // 2)
+            weights = softmax(
+                [
+                    jnp.where(same, dot(pair_of(0, pair), pair_of(1, pair), NTDOT), -1e30)
+                    for pair in pairs
+                ]
+            )
+            for pair, weight in zip(pairs, weights):
+                result = dot(weight, pair_of(2, pair), NNDOT).astype(jnp.bfloat16)
+                otmp[:, pl.ds(2 * pair, 2), :, :] = result.reshape(4, 2, GP, HD)
+            rows = pl.ds(pl.multiple_of(jj * GP, GP), GP)
+            for fb in (0, 2):
+                pieces = swap(
+                    otmp[fb].reshape(GP * GP, HD), otmp[fb + 1].reshape(GP * GP, HD)
+                )
+                for k in range(2):
+                    osend[c, pl.ds((fb + k) * GP, GP), rows, :] = pieces[k].reshape(GP, GP, HD)
+            return carry
+
+        lax.fori_loop(0, JC, temporal, 0)
+
+        def reply(i, carry):
+            d = frame_of(i)
+            remote(
+                osend.at[c, d], orecv.at[c, f // 2, f % 2], os_sem.at[c], or_sem.at[c], (g, d)
+            ).start()
+            return carry
+
+        lax.fori_loop(1, FRAMES, reply, 0)
+        pltpu.make_async_copy(
+            osend.at[c, f], orecv.at[c, f // 2, f % 2], own_sem.at[NC + c]
+        ).start()
+
+    def temporal_block(c):
+        block = att.at[g, :, pl.ds(HALF + c * 2 * JC * HD, 2 * JC * HD)]
+        return remote(block, block, part_s.at[2 + c], part_r.at[2 + c], partner)
+
+    def collect(c):
         wait_bytes(osend.at[c, pl.ds(0, FRAMES - 1)], or_sem.at[c])
         pltpu.make_async_copy(
             osend.at[c, f], orecv.at[c, f // 2, f % 2], own_sem.at[NC + c]
@@ -319,32 +356,45 @@
             hh, jj = i // JC, i % JC
             lanes = pl.ds(HALF + (c * 2 * JC + i) * HD, HD)
             att[g, :, lanes] = orecv[c, :, hh, pl.ds(jj * GP, GP), :].reshape(ROWS, HD)
-        block = att.at[g, :, pl.ds(HALF + c * 2 * JC * HD, 2 * JC * HD)]
-        remote(block, block, part_s.at[2 + c], part_r.at[2 + c], partner).start()
-
+        temporal_block(c).start()
+
+    arrive(0)
+    attend(0)
+    arrive(1)
+    attend(1)
+    for part in range(3):
+        wait_bytes(wb.at[part, 0, pl.ds(0, 3)], w2r.at[part])
+    post_direct(0, 0)
+    post_direct(1, 0)
+    post_direct(2, 0)
+    post_direct(0, 1)
+    post_direct(1, 1)
+    post_direct(2, 1)
+    collect(0)
+    post_direct(0, 2)
+    post_direct(1, 2)
+    post_direct(2, 2)
+    post_direct(0, 3)
+    collect(1)
+    pass_on(0, 0)
+    pass_on(1, 0)
+    pass_on(2, 0)
+    post_direct(1, 3)
+    post_direct(2, 3)
+    pass_on(0, 1)
+    pass_on(1, 1)
+    pass_on(2, 1)
     hid_in.wait()
     hid_out.wait_recv()
     att_s.wait_recv()
     for c in range(NC):
-        block = att.at[g, :, pl.ds(HALF + c * 2 * JC * HD, 2 * JC * HD)]
-        remote(block, block, part_s.at[2 + c], part_r.at[2 + c], partner).wait_recv()
-
-    for part in (1, 2):
-        pass_on(part, 0)
-        post_direct(part, 2)
-    for r in range(2):
-        pass_on(0, r)
+        temporal_block(c).wait_recv()
 
     def project(r, carry):
-        @pl.when(r < 4)
+        @pl.when((r == 2) | (r == 3))
         def _():
             for part in (1, 2):
                 pass_on(part, r)
-
-        @pl.when(r == 1)
-        def _():
-            for part in (1, 2):
-                post_direct(part, 3)
 
         @pl.when(r == 2)
         def _():
@@ -408,8 +458,7 @@
     for c in w1 + w2:
         c.wait_send()
     for c in range(NC):
-        block = att.at[g, :, pl.ds(HALF + c * 2 * JC * HD, 2 * JC * HD)]
-        remote(block, block, part_s.at[2 + c], part_r.at[2 + c], partner).wait_send()
+        temporal_block(c).wait_send()
         wait_bytes(recv.at[c, pl.ds(0, FRAMES - 1)], qs_sem.at[c])
         wait_bytes(osend.at[c, pl.ds(0, FRAMES - 1)], os_sem.at[c])
 
@@ -459,8 +508,8 @@
             pltpu.VMEM((3, 4, 4, 4, COLS, PART), bf16),
             pltpu.VMEM((PLANE, D), bf16),
             pltpu.VMEM((2, ROWS, HALF), bf16),
-            pltpu.VMEM((3, FRAMES * GP, HD), f32),
-            pltpu.VMEM((FRAMES * GP, HD), f32),
+            pltpu.VMEM((3, 4, GP, GP, HD), bf16),
+            pltpu.VMEM((4, GP, GP, HD), bf16),
             pltpu.VMEM((2, 96, HALF), bf16),
             pltpu.VMEM((2, 2, 32, HD), f32),
             pltpu.VMEM((96, 2 * ROWS), f32),
@@ -471,6 +520,9 @@
             dma((9,)), dma((3,)), dma((9,)), dma((3,)),
             dma((3, 4, 4)), dma((3, 4, 4)),
             dma((5,)), dma((5,)),
+            pltpu.SemaphoreType.REGULAR,
+            pltpu.SMEM((H,), jnp.int32),
+            pltpu.VMEM((GP * GP, GP * GP), bf16),
         ],
         compiler_params=pltpu.CompilerParams(
             collective_id=0, has_side_effects=True, vmem_limit_bytes=62 * 2**20
@@ -480,7 +532,7 @@
         ),
         name="guided_layer",
     )(
-        order_of(head_labels), queries, key_heads, value_heads, hidden_state,
+        head_labels, queries, key_heads, value_heads, hidden_state,
         out_weight.T, final_weight.T, gate_scale, final_scale, final_shift,
     )
     return (latent.T - euler_step * guided).T

time: 132 us -> 128 us (0.970)
  other arithmetic: 3.54 us -> 1.48 us
    reduce_sum x2 -> x0, other arithmetic: 1.4 us -> none  [the longest x1 0.77 us: order_of(): jnp.sum(jnp.where(index[None, :] < index[:, None], labels[None, :], 0), a...]
where the time goes in v2:
time: 128 us
  Pallas kernels  127 us (99%)
  other arithmetic  1.48 us (1%)
    pallas_call x1, Pallas kernels, per_device(): pl.pallas_call(kernel, out_shape=jax.ShapeDtypeStruct((OUT_CH // 2, ROWS)...  127 us

profile of v2, /device:TPU:1, one launch (start us, length us, event | category | flops | bytes accessed | tf_op | source)
XLA Modules:
  0.0 128.3 jit_solution(5122551450935508970)
XLA Ops:
  0.0 0.0 copy-start
  0.0 126.8 %guided_layer.1 = f32[32,512]{1,0:T(8,128)} custom-call(s32[24]{0:T(128)} %labels.1, bf16[1,512,3072]{2,1,0:T(8,128)(2,1)} %q_hbm.1, bf16[1,512,3072]{2,1,0:T(8,128)(2,1)} %k_hbm.1, bf16[1,512,3072]{2,1,0:T(8,128)(2,1)} %v_hbm.1, bf16[1,512,3072]{2,1,0:T(8,128)(2,1)} %hid_hbm.1, bf16[24,3072]{1,0:T(8,128)(2,1)} %bitcast.9, bf16[64,3072]{1,0:T(8,128)(2,1)} %bitcast.8, ...), custom_call_target="tpu_custom_call" | custom-call | flops 16000000000 | bytes 20000000 | tf_op jit(solution)/shard_map/guided_layer/pallas_call | solution.py:493
  126.8 0.0 copy-done
  126.8 1.5 %fusion = f32[512,32]{0,1:T(8,128)} fusion(f32[512,32]{0,1:T(8,128)S(1)} %copy-done, f32[32,512]{1,0:T(8,128)} %guided_layer.1), kind=kLoop, calls=%fused_computation.1 | loop fusion | flops 32768 | bytes 196608 | tf_op jit(solution)/shard_map/transpose | solution.py:538
Async XLA Ops:
  0.0 126.8 %copy-start = (f32[512,32]{0,1:T(8,128)S(1)}, f32[512,32]{0,1:T(8,128)}, u32[]{:S(2)}) copy-start(f32[512,32]{0,1:T(8,128)} %param.21) | copy-start | bytes 196612

commit v3 on v2

--- a/solution.py
+++ b/solution.py
@@ -181,7 +181,6 @@
     gather(1)
     pl.semaphore_wait(step_sem, 3)
     post(0)
-    post(1)
     w2 = []
     for part in range(3):
         wait_bytes(wb.at[part, 0, 0, pl.ds(0, 3)], w1r.at[part])
@@ -191,6 +190,7 @@
             c.start()
             w2.append(c)
 
+    post(1)
 
     def softmax(blocks):
         tops = [jnp.max(v, axis=-1, keepdims=True) for v in blocks]
@@ -361,29 +361,29 @@
     arrive(0)
     attend(0)
     arrive(1)
-    attend(1)
     for part in range(3):
         wait_bytes(wb.at[part, 0, pl.ds(0, 3)], w2r.at[part])
     post_direct(0, 0)
     post_direct(1, 0)
     post_direct(2, 0)
+    attend(1)
     post_direct(0, 1)
     post_direct(1, 1)
     post_direct(2, 1)
-    collect(0)
+    pass_on(0, 0)
+    pass_on(1, 0)
+    pass_on(2, 0)
     post_direct(0, 2)
     post_direct(1, 2)
     post_direct(2, 2)
     post_direct(0, 3)
-    collect(1)
-    pass_on(0, 0)
-    pass_on(1, 0)
-    pass_on(2, 0)
-    post_direct(1, 3)
-    post_direct(2, 3)
+    collect(0)
     pass_on(0, 1)
     pass_on(1, 1)
     pass_on(2, 1)
+    post_direct(1, 3)
+    post_direct(2, 3)
+    collect(1)
     hid_in.wait()
     hid_out.wait_recv()
     att_s.wait_recv()
@@ -438,6 +438,24 @@
         zacc[pl.ds(base, 8), :] = jnp.where(pick, squares, block)
     zsend = remote(zacc.at[pl.ds(48, 48)], zrecv, part_s.at[4], part_r.at[4], partner)
     zsend.start()
+    hid_out.wait_send()
+    att_s.wait_send()
+    for c in w1 + w2:
+        c.wait_send()
+    for c in range(NC):
+        temporal_block(c).wait_send()
+        wait_bytes(recv.at[c, pl.ds(0, FRAMES - 1)], qs_sem.at[c])
+        wait_bytes(osend.at[c, pl.ds(0, FRAMES - 1)], os_sem.at[c])
+
+    def drain(r, carry):
+        for part in range(3):
+            for way in range(2):
+                direct(part, r, way).wait_send()
+                forward(part, r, way).wait_send()
+        return carry
+
+    lax.fori_loop(0, 4, drain, 0)
+
     zsend.wait_recv()
     velocity = []
     for b in range(2):
@@ -451,25 +469,7 @@
             + consts[b, 1, :, 0:1]
         )
     out[...] = velocity[1] + guidance * (velocity[0] - velocity[1])
-
     zsend.wait_send()
-    hid_out.wait_send()
-    att_s.wait_send()
-    for c in w1 + w2:
-        c.wait_send()
-    for c in range(NC):
-        temporal_block(c).wait_send()
-        wait_bytes(recv.at[c, pl.ds(0, FRAMES - 1)], qs_sem.at[c])
-        wait_bytes(osend.at[c, pl.ds(0, FRAMES - 1)], os_sem.at[c])
-
-    def drain(r, carry):
-        for part in range(3):
-            for way in range(2):
-                direct(part, r, way).wait_send()
-                forward(part, r, way).wait_send()
-        return carry
-
-    lax.fori_loop(0, 4, drain, 0)
 
 
 def per_device(

time: 128 us -> 128 us (level)
  no operation moved by 1% of the time
where the time goes in v3:
time: 128 us
  Pallas kernels  126 us (98%)
  other arithmetic  1.48 us (1%)
    pallas_call x1, Pallas kernels, per_device(): pl.pallas_call(kernel, out_shape=jax.ShapeDtypeStruct((OUT_CH // 2, ROWS)...  126 us

profile of v3, /device:TPU:1, one launch (start us, length us, event | category | flops | bytes accessed | tf_op | source)
XLA Modules:
  0.0 127.9 jit_solution(8784494877235973020)
XLA Ops:
  0.0 0.0 copy-start
  0.0 126.4 %guided_layer.1 = f32[32,512]{1,0:T(8,128)} custom-call(s32[24]{0:T(128)} %labels.1, bf16[1,512,3072]{2,1,0:T(8,128)(2,1)} %q_hbm.1, bf16[1,512,3072]{2,1,0:T(8,128)(2,1)} %k_hbm.1, bf16[1,512,3072]{2,1,0:T(8,128)(2,1)} %v_hbm.1, bf16[1,512,3072]{2,1,0:T(8,128)(2,1)} %hid_hbm.1, bf16[24,3072]{1,0:T(8,128)(2,1)} %bitcast.9, bf16[64,3072]{1,0:T(8,128)(2,1)} %bitcast.8, ...), custom_call_target="tpu_custom_call" | custom-call | flops 16000000000 | bytes 20000000 | tf_op jit(solution)/shard_map/guided_layer/pallas_call | solution.py:493
  126.4 0.0 copy-done
  126.5 1.5 %fusion = f32[512,32]{0,1:T(8,128)} fusion(f32[512,32]{0,1:T(8,128)S(1)} %copy-done, f32[32,512]{1,0:T(8,128)} %guided_layer.1), kind=kLoop, calls=%fused_computation.1 | loop fusion | flops 32768 | bytes 196608 | tf_op jit(solution)/shard_map/transpose | solution.py:538
Async XLA Ops:
  0.0 126.4 %copy-start = (f32[512,32]{0,1:T(8,128)S(1)}, f32[512,32]{0,1:T(8,128)}, u32[]{:S(2)}) copy-start(f32[512,32]{0,1:T(8,128)} %param.21) | copy-start | bytes 196612

commit v4 on v3

--- a/solution.py
+++ b/solution.py
@@ -366,10 +366,10 @@
     post_direct(0, 0)
     post_direct(1, 0)
     post_direct(2, 0)
-    attend(1)
     post_direct(0, 1)
     post_direct(1, 1)
     post_direct(2, 1)
+    attend(1)
     pass_on(0, 0)
     pass_on(1, 0)
     pass_on(2, 0)

time: 128 us -> 128 us (level)
  no operation moved by 1% of the time
where the time goes in v4:
time: 128 us
  Pallas kernels  126 us (98%)
  other arithmetic  1.48 us (1%)
    pallas_call x1, Pallas kernels, per_device(): pl.pallas_call(kernel, out_shape=jax.ShapeDtypeStruct((OUT_CH // 2, ROWS)...  126 us

profile of v4, /device:TPU:1, one launch (start us, length us, event | category | flops | bytes accessed | tf_op | source)
XLA Modules:
  0.0 127.9 jit_solution(16491318361936795465)
XLA Ops:
  0.0 0.0 copy-start
  0.0 126.4 %guided_layer.1 = f32[32,512]{1,0:T(8,128)} custom-call(s32[24]{0:T(128)} %labels.1, bf16[1,512,3072]{2,1,0:T(8,128)(2,1)} %q_hbm.1, bf16[1,512,3072]{2,1,0:T(8,128)(2,1)} %k_hbm.1, bf16[1,512,3072]{2,1,0:T(8,128)(2,1)} %v_hbm.1, bf16[1,512,3072]{2,1,0:T(8,128)(2,1)} %hid_hbm.1, bf16[24,3072]{1,0:T(8,128)(2,1)} %bitcast.9, bf16[64,3072]{1,0:T(8,128)(2,1)} %bitcast.8, ...), custom_call_target="tpu_custom_call" | custom-call | flops 16000000000 | bytes 20000000 | tf_op jit(solution)/shard_map/guided_layer/pallas_call | solution.py:493
  126.4 0.0 copy-done
  126.5 1.5 %fusion = f32[512,32]{0,1:T(8,128)} fusion(f32[512,32]{0,1:T(8,128)S(1)} %copy-done, f32[32,512]{1,0:T(8,128)} %guided_layer.1), kind=kLoop, calls=%fused_computation.1 | loop fusion | flops 32768 | bytes 196608 | tf_op jit(solution)/shard_map/transpose | solution.py:538
Async XLA Ops:
  0.0 126.4 %copy-start = (f32[512,32]{0,1:T(8,128)S(1)}, f32[512,32]{0,1:T(8,128)}, u32[]{:S(2)}) copy-start(f32[512,32]{0,1:T(8,128)} %param.21) | copy-start | bytes 196612
